TPU v7x, 32 devices: a whole 2x2x4 slice. The times are simulated.
32 devices in a mesh: ctx: 16 (over z, y, core), grp: 2 (over x).
Axes of the slice: x: 2, y: 2, z: 4, core: 2. Of those that a mesh axis runs over, the one named last changes fastest.
Arguments:
- queries: bfloat16 [2048, 1024], P('ctx', 'grp'), may hold values from -6 to 6
- keys: bfloat16 [2048, 1024], P('ctx', 'grp'), may hold values from -6 to 6
- values: bfloat16 [2048, 1024], P('ctx', 'grp'), may hold values from -6 to 6
- block_order: int32 [32], replicated, may hold values from 0 to 31, each once
- token_ids: int32 [2048], P('ctx'), may hold values from 0 to 511
- stream_table: bfloat16 [4, 512, 2048], P(None, None, 'grp'), may hold values from -70 to 70
- short_filter: float32 [3, 7, 2048], P(None, None, 'grp'), may hold values from -2 to 2
- long_filter: bfloat16 [128, 128], P('grp'), may hold values from -0.5 to 0.5
- norm_gain: float32 [2048], P('grp'), may hold values from 0.1 to 1.9
Outputs:
- attended: bfloat16 [2048, 1024], P('ctx', 'grp')
- hyena_out: bfloat16 [2048, 2048], P('ctx', 'grp')
All inputs are finite; a program needn't handle non-finite values.
Results may differ from a plain program's by a relative error of at most 0.004.
Values may be sent and summed in bfloat16 or wider, within the bound.
A program may use at most 128 MiB of HBM per device.

v0:
```python
import math

import jax
import jax.numpy as jnp
from jax import lax
from jax.sharding import PartitionSpec as P

HD = 128


neg_fill = -1e30
eps_norm = 1e-06


def passed_along(block, axis, distance):
    devices = range(lax.axis_size(axis))
    route = [(i - distance, i) for i in devices if i - distance in devices]
    return lax.ppermute(block, axis, route)


def block_positions(order, row_index, row_count):
    half_rows = row_count // 2
    slot = 2 * (row_index // row_count) + row_index % row_count // half_rows
    hits = slot[:, None] == jnp.arange(order.shape[0], dtype=jnp.int32)[None, :]
    block_start = jnp.sum(jnp.where(hits, order[None, :], 0), axis=1)
    return block_start * half_rows + row_index % half_rows


def attend_tile(running, keys_tile, values_tile, key_pos, query_heads, query_pos, score_scale):
    row_peak, row_total, weighted = running
    scores = (
        jnp.einsum("qhd,khd->hqk", query_heads, keys_tile, preferred_element_type=jnp.float32)
        * score_scale
    )
    visible = (key_pos[None, :] <= query_pos[:, None])[None]
    scores = jnp.where(visible, scores, neg_fill)
    new_peak = jnp.maximum(row_peak, jnp.max(scores, axis=2))
    weights = jnp.where(visible, jnp.exp(scores - new_peak[:, :, None]), 0.0)
    rescale = jnp.exp(row_peak - new_peak)
    row_total = row_total * rescale + jnp.sum(weights, axis=2)
    weighted = weighted * rescale.T[:, :, None] + jnp.einsum(
        "hqk,khd->qhd",
        weights.astype(jnp.bfloat16),
        values_tile,
        preferred_element_type=jnp.float32,
    )
    return (new_peak, row_total, weighted)


def guarded_tile(running, keys_tile, values_tile, key_pos, query_heads, query_pos, score_scale):
    return attend_tile(
        running, keys_tile, values_tile, key_pos, query_heads, query_pos, score_scale
    )


def lookup_rows(id_rows, stream_table):
    vocab_size = stream_table.shape[1]
    one_hot = (id_rows[:, None] == jnp.arange(vocab_size, dtype=jnp.int32)[None, :]).astype(
        jnp.bfloat16
    )
    return jnp.einsum("rv,svc->src", one_hot, stream_table, preferred_element_type=jnp.float32)


def short_mix(features, short_filter, out_rows):
    lead_rows = short_filter.shape[1] - 1
    results = []
    for stream in range(3):
        running = jnp.zeros((out_rows, features.shape[2]), jnp.float32)
        for lag_step in range(lead_rows + 1):
            running = (
                running
                + short_filter[stream, lag_step][None, :]
                * features[stream + 1, lead_rows - lag_step : lead_rows - lag_step + out_rows]
            )
        results.append(running)
    return results


def long_mix(extended, long_filter, out_rows):
    group_count, tap_count = long_filter.shape
    span_rows = extended.shape[0]
    lag_table = (
        jnp.arange(out_rows, dtype=jnp.int32)[:, None]
        + (tap_count - 1)
        - jnp.arange(span_rows, dtype=jnp.int32)[None, :]
    )
    inside = (lag_table >= 0) & (lag_table < tap_count)
    picked = long_filter[:, jnp.clip(lag_table, 0, tap_count - 1)]
    toeplitz = jnp.where(inside[None], picked, jnp.zeros((), long_filter.dtype))
    grouped = extended.reshape(span_rows, group_count, -1)
    result = jnp.einsum("gts,sgc->tgc", toeplitz, grouped, preferred_element_type=jnp.float32)
    return result.reshape(out_rows, -1)


def body(
    queries,
    keys,
    values,
    block_order,
    token_ids,
    stream_table,
    short_filter,
    long_filter,
    norm_gain,
):
    row_count = queries.shape[0]
    head_count = queries.shape[1] // HD
    device_index = lax.axis_index("ctx")
    query_pos = block_positions(
        block_order, device_index * row_count + jnp.arange(row_count, dtype=jnp.int32), row_count
    )
    query_heads = queries.reshape(row_count, head_count, HD)
    score_scale = 1.0 / math.sqrt(HD)
    initial = (
        jnp.full((head_count, row_count), neg_fill, jnp.float32),
        jnp.zeros((head_count, row_count), jnp.float32),
        jnp.zeros((row_count, head_count, HD), jnp.float32),
    )
    running = initial
    keys_piece = lax.all_gather(keys, "ctx", axis=0, tiled=True)
    values_piece = lax.all_gather(values, "ctx", axis=0, tiled=True)
    key_count = keys_piece.shape[0]
    key_pos_all = block_positions(block_order, jnp.arange(key_count, dtype=jnp.int32), row_count)
    keys_all = keys_piece.reshape(key_count, head_count, HD)
    values_all = values_piece.reshape(key_count, head_count, HD)
    tile_rows = 1024

    def one_tile(state, tile_index):
        first_key = tile_index * tile_rows
        keys_tile = lax.dynamic_slice_in_dim(keys_all, first_key, tile_rows, 0)
        values_tile = lax.dynamic_slice_in_dim(values_all, first_key, tile_rows, 0)
        key_pos = lax.dynamic_slice_in_dim(key_pos_all, first_key, tile_rows, 0)
        return (
            guarded_tile(
                state, keys_tile, values_tile, key_pos, query_heads, query_pos, score_scale
            ),
            None,
        )

    running, unused = lax.scan(
        one_tile, running, jnp.arange(key_count // tile_rows, dtype=jnp.int32)
    )
    row_peak, row_total, weighted = running
    attended = (
        (weighted / row_total.T[:, :, None])
        .astype(jnp.bfloat16)
        .reshape(row_count, head_count * HD)
    )
    token_count = token_ids.shape[0]
    lead_rows = short_filter.shape[1] - 1
    tap_count = long_filter.shape[1]
    first_row = device_index * token_count
    rim_ids = passed_along(token_ids[token_count - lead_rows :], "ctx", 1)
    id_rows = jnp.concatenate([rim_ids, token_ids])
    span_start = first_row - lead_rows
    features = lookup_rows(id_rows, stream_table)
    placed = span_start + jnp.arange(id_rows.shape[0], dtype=jnp.int32)
    features = features * (placed >= 0).astype(jnp.float32)[None, :, None]
    first_mix, second_mix, third_mix = short_mix(features, short_filter, token_count)
    product = (first_mix * third_mix).astype(jnp.bfloat16)
    product_rim = passed_along(product[token_count - (tap_count - 1) :], "ctx", 1)
    extended = jnp.concatenate([product_rim, product])
    residual = features[0, id_rows.shape[0] - token_count :]
    convolved = long_mix(extended, long_filter, token_count)
    mixed = residual + second_mix * convolved
    square_sum = lax.psum(jnp.sum(mixed * mixed, axis=1), "grp")
    channel_total = mixed.shape[1] * lax.axis_size("grp")
    inverse_rms = lax.rsqrt(square_sum / channel_total + eps_norm)
    hyena_out = (mixed * norm_gain[None, :] * inverse_rms[:, None]).astype(jnp.bfloat16)
    return (attended, hyena_out)


def solution(mesh):
    placed = (
        P("ctx", "grp"),
        P("ctx", "grp"),
        P("ctx", "grp"),
        P(),
        P("ctx"),
        P(None, None, "grp"),
        P(None, None, "grp"),
        P("grp", None),
        P("grp"),
    )
    return jax.shard_map(
        body,
        mesh=mesh,
        in_specs=placed,
        out_specs=(P("ctx", "grp"), P("ctx", "grp")),
        check_vma=False,
    )
```

profile of v0, /device:TPU:0, one launch (start us, length us, event | category | flops | bytes accessed | tf_op | source)
XLA Modules:
  0.0 152.5 jit_solution(10545052957274096014)
XLA Ops:
  7.2 0.7 all-gather.5.cloned.1.call-update
  7.9 0.7 slice.135
  8.7 2.3 %collective-permute-start = (s32[6]{0:T(128)S(1)}, s32[6]{0:T(128)S(1)}, u32[]{:S(2)}, u32[]{:S(2)}) collective-permute-start(s32[6]{0:T(128)S(1)} %slice.135), channel_id=1, source_target_pairs={{0,2},{2,4},{4,6},{6,8},{8,10},{10,12},{12,14},{14,16},{16,18},{18... | collective-permute-start | bytes 80 | tf_op jit(solution)/shard_map/ppermute | solution.py:18
  11.0 1.7 %copy.30 = bf16[128,512]{0,1:T(8,128)(2,1)} copy(bf16[128,512]{1,0:T(8,128)(2,1)} %param.12) | data formatting | bytes 262144 | tf_op args[1]
  12.9 0.7 select_reduce_fusion.1
  13.6 0.3 reshape.246
  14.0 0.8 select_reduce_fusion
  14.8 0.8 fusion.97
  15.6 1.4 fusion.96
  17.1 0.7 pad_add_fusion
  17.8 3.0 %multiply_bitcast_fusion = f32[4,134,1024]{2,1,0:T(8,128)S(1)} fusion(bf16[4,512,1024]{2,1,0:T(8,128)(2,1)} %param.16, f32[134]{0:T(256)S(1)} %compare_convert_fusion, s32[134]{0:T(256)S(1)} %pad_add_fusion), kind=kOutput, calls=%fused_computation.32 | convolution fusion | flops 562654208 | bytes 6390832 | tf_op jit(solution)/shard_map/rv,svc->src/dot_general | solution.py:61
  20.8 0.9 fusion.28
  21.8 4.6 %collective-permute-start.1 = (bf16[127,1024]{1,0:T(8,128)(2,1)S(1)}, bf16[127,1024]{1,0:T(8,128)(2,1)S(1)}, u32[]{:S(2)}, u32[]{:S(2)}) collective-permute-start(bf16[127,1024]{1,0:T(8,128)(2,1)S(1)} %slice.204), channel_id=1, source_target_pairs={{0,2},{2,4},{4,6},{6,8},{8,10},{10,12},{12,14},{14,16},{16,18},{18... | collective-permute-start | bytes 780296 | tf_op jit(solution)/shard_map/ppermute | solution.py:18
  26.6 66.2 %gather_fusion = bf16[32640,64]{1,0:T(8,128)(2,1)} fusion(bf16[64,128]{0,1:T(8,128)(2,1)S(1)} %copy.37, s32[32768]{0:T(1024)S(1)} %pad_clamp_fusion), kind=kCustom, calls=%fused_computation | custom fusion | bytes 8486400 | tf_op jit(solution)/shard_map/gather | solution.py:88
  92.8 8.6 %copy.38 = bf16[32640,64]{0,1:T(8,128)(2,1)} copy(bf16[32640,64]{1,0:T(8,128)(2,1)} %gather_fusion) | data formatting | bytes 8355840 | tf_op jit(solution)/shard_map/gather | solution.py:88
  101.4 15.9 %reshape.249 = bf16[128,255,64]{1,0,2:T(8,128)(2,1)} reshape(bf16[32640,64]{0,1:T(8,128)(2,1)} %copy.38) | data formatting | bytes 8355840 | tf_op jit(solution)/shard_map/gather | solution.py:88
  117.7 1.0 copy.36
  118.7 3.5 %fusion.20 = f32[64,16,128]{2,1,0:T(8,128)S(1)} fusion(bf16[255,64,16]{0,2,1:T(8,128)(2,1)} %bitcast.258, bf16[128,255,64]{1,0,2:T(8,128)(2,1)} %reshape.249, pred[128,255]{1,0:T(8,128)(4,1)S(1)} %fusion.73), kind=kOutput, calls=%fused_computation.28 | convolution fusion | flops 68935680 | bytes 5257088 | tf_op jit(solution)/shard_map/gts,sgc->tgc/dot_general | solution.py:91
  122.5 0.6 multiply_reduce_fusion
  123.1 4.9 %psum.7 = f32[128]{0:T(128)S(1)} all-reduce(f32[128]{0:T(128)S(1)} %get-tuple-element.132), channel_id=1, replica_groups=mesh['ctx'=16,'grp'=2] {'grp'}, use_global_device_ids=true, to_apply=%region_7.8 | all-reduce | flops 128 | bytes 1024 | tf_op jit(solution)/shard_map/psum | solution.py:166
  128.1 0.8 multiply_convert_fusion
  128.9 4.0 %copy.32 = bf16[2048,512]{0,1:T(8,128)(2,1)} copy(bf16[2048,512]{1,0:T(8,128)(2,1)} %all-gather.5.cloned.1.call-done) | data formatting | bytes 4194304 | tf_op jit(solution)/shard_map/all_gather | solution.py:121
  132.9 11.9 %while.15 = (s32[]{:T(128)}, f32[4,128]{1,0:T(4,128)S(1)}, f32[4,128]{1,0:T(4,128)S(1)}, f32[128,4,128]{0,2,1:T(8,128)S(1)}, s32[2]{0:T(128)S(1)}, /*index=5*/s3...) while((s32[]{:T(128)}, f32[4,128]{1,0:T(4,128)S(1)}, ...), condition=%wide.region_5.6_spmd.clone, body=%wide.region_2.5_spmd.clone.sunk | while | flops 275581952 | bytes 9614039 | solution.py:140
  132.9 0.6 dynamic_slice.29
  134.4 1.9 %fusion.112 = (f32[4,128]{1,0:T(4,128)S(1)}, f32[4,1024,128]{2,1,0:T(8,128)S(1)}) fusion(pred[128,1024]{0,1:T(8,128)(4,1)S(1)} %broadcast_compare_fusion.2, bf16[128,4,128]{2,0,1:T(8,128)(2,1)S(1)} %get-tuple-element.262, bf16[2048,4,128]{0,2,1:T(8,128)(2,1)} %get-tuple-element.261, s32[]{:T(128)S(6)} %select_n.185), kind=kOutput, calls=%fused_computation.3.clone.1 | convolution fusion | flops 135790080 | bytes 3409924 | tf_op jit(solution)/shard_map/while/body/eval_jaxpr/qhd,khd->hqk/dot_general | solution.py:32
  136.3 2.0 %fusion.116 = f32[128,4,128]{0,2,1:T(8,128)S(1)} fusion(f32[4,1024,128]{2,1,0:T(8,128)S(1)} %get-tuple-element.224, bf16[2048,4,128]{0,2,1:T(8,128)(2,1)} %get-tuple-element.263, s32[]{:T(128)S(6)} %select_n.185, f32[4,128]{1,0:T(4,128)S(1)} %get-tuple-element.255, pred[128,1024]{0,1:T(8,128)(4,1)S(1)} %broadcast_compare_fusion.2, ...), kind=kOutput, calls=%fused_computation.7.clone.1 | convolution fusion | flops 137035776 | bytes 3805189 | tf_op jit(solution)/shard_map/while/body/eval_jaxpr/hqk,khd->qhd/dot_general | solution.py:41
  138.3 0.5 fusion.114
  138.9 0.6 dynamic_slice.29
  140.3 1.9 %fusion.112 = (f32[4,128]{1,0:T(4,128)S(1)}, f32[4,1024,128]{2,1,0:T(8,128)S(1)}) fusion(pred[128,1024]{0,1:T(8,128)(4,1)S(1)} %broadcast_compare_fusion.2, bf16[128,4,128]{2,0,1:T(8,128)(2,1)S(1)} %get-tuple-element.262, bf16[2048,4,128]{0,2,1:T(8,128)(2,1)} %get-tuple-element.261, s32[]{:T(128)S(6)} %select_n.185), kind=kOutput, calls=%fused_computation.3.clone.1 | convolution fusion | flops 135790080 | bytes 3409924 | tf_op jit(solution)/shard_map/while/body/eval_jaxpr/qhd,khd->hqk/dot_general | solution.py:32
  142.2 2.0 %fusion.116 = f32[128,4,128]{0,2,1:T(8,128)S(1)} fusion(f32[4,1024,128]{2,1,0:T(8,128)S(1)} %get-tuple-element.224, bf16[2048,4,128]{0,2,1:T(8,128)(2,1)} %get-tuple-element.263, s32[]{:T(128)S(6)} %select_n.185, f32[4,128]{1,0:T(4,128)S(1)} %get-tuple-element.255, pred[128,1024]{0,1:T(8,128)(4,1)S(1)} %broadcast_compare_fusion.2, ...), kind=kOutput, calls=%fused_computation.7.clone.1 | convolution fusion | flops 137035776 | bytes 3805189 | tf_op jit(solution)/shard_map/while/body/eval_jaxpr/hqk,khd->qhd/dot_general | solution.py:41
  144.2 0.5 fusion.114
  144.9 0.8 copy.41
  (46 shorter events, 1.7 us)
Async XLA Ops:
  7.2 121.7 %all-gather.5.cloned.1.call-start = ((), (), s32[]{:S(2)}) async-start(), calls=%async_computation.1 | async-start | bytes 2228224 | tf_op jit(solution)/shard_map/all_gather | solution.py:121
  7.9 125.0 %all-gather.3.cloned.1.call-start = ((), (), s32[]{:S(2)}) async-start(), calls=%async_computation | async-start | bytes 2228224 | tf_op jit(solution)/shard_map/all_gather | solution.py:120
  8.7 8.4 %collective-permute-start = (s32[6]{0:T(128)S(1)}, s32[6]{0:T(128)S(1)}, u32[]{:S(2)}, u32[]{:S(2)}) collective-permute-start(s32[6]{0:T(128)S(1)} %slice.135), channel_id=1, source_target_pairs={{0,2},{2,4},{4,6},{6,8},{8,10},{10,12},{12,14},{14,16},{16,18},{18... | collective-permute-start | bytes 80 | tf_op jit(solution)/shard_map/ppermute | solution.py:18
  20.8 5.6 %copy-start.2 = (bf16[64,128]{1,0:T(8,128)(2,1)S(1)}, bf16[64,128]{1,0:T(8,128)(2,1)}, u32[]{:S(2)}) copy-start(bf16[64,128]{1,0:T(8,128)(2,1)} %param.18) | copy-start | bytes 49156
  21.8 95.9 %collective-permute-start.1 = (bf16[127,1024]{1,0:T(8,128)(2,1)S(1)}, bf16[127,1024]{1,0:T(8,128)(2,1)S(1)}, u32[]{:S(2)}, u32[]{:S(2)}) collective-permute-start(bf16[127,1024]{1,0:T(8,128)(2,1)S(1)} %slice.204), channel_id=1, source_target_pairs={{0,2},{2,4},{4,6},{6,8},{8,10},{10,12},{12,14},{14,16},{16,18},{18... | collective-permute-start | bytes 780296 | tf_op jit(solution)/shard_map/ppermute | solution.py:18
  101.4 15.9 %copy-start.1 = (bf16[128,512]{1,0:T(8,128)(2,1)S(1)}, bf16[128,512]{1,0:T(8,128)(2,1)}, u32[]{:S(2)}) copy-start(bf16[128,512]{1,0:T(8,128)(2,1)} %param.11) | copy-start | bytes 393220
  122.5 5.6 %copy-start.3 = (f32[1024]{0:T(1024)S(1)}, f32[1024]{0:T(1024)}, u32[]{:S(2)}) copy-start(f32[1024]{0:T(1024)} %param.19) | copy-start | bytes 12292
  128.9 4.0 %copy-start = (f32[128,4,128]{0,2,1:T(8,128)S(1)}, f32[128,4,128]{0,2,1:T(8,128)}, u32[]{:S(2)}) copy-start(f32[128,4,128]{0,2,1:T(8,128)} %custom-call.2) | copy-start | bytes 786436
Sparse Core Ops, SparseCore 0:
  10.2 44.1 all-gather.4
  57.1 39.9 all-gather.2
where the time goes:
time: 153 us; the launch traced here: 152 us
  local copies, waits for them, and re-layouts  103 us (67%)
  matrix products  14.3 us (9%)
  between operations  14.3 us (9%)
  starting transfers between devices  7.03 us (5%)
  other arithmetic  6.48 us (4%)
  blocking collectives  4.93 us (3%)
    gather x3, local copies, waits for them, and re-layouts, long_mix(): picked = long_filter[:, jnp.clip(lag_table, 0, tap_count - 1)]  90.7 us
    ppermute x2, starting transfers between devices, passed_along(): return lax.ppermute(block, axis, route)  6.96 us
    psum x1, blocking collectives, body(): square_sum = lax.psum(jnp.sum(mixed * mixed, axis=1), 'grp')  4.93 us
    dot_general x2, matrix products, attend_tile(): jnp.einsum('hqk,khd->qhd', weights.astype(jnp.bfloat16), values_tile, pre...  4.06 us
    all_gather x1, local copies, waits for them, and re-layouts, body(): values_piece = lax.all_gather(values, 'ctx', axis=0, tiled=True)  4 us
    dot_general x2, matrix products, attend_tile(): jnp.einsum('qhd,khd->hqk', query_heads, keys_tile, preferred_element_type...  3.7 us
    dot_general x1, matrix products, long_mix(): jnp.einsum('gts,sgc->tgc', toeplitz, grouped, preferred_element_type=jnp....  3.53 us
  transfers between devices with their start and end apart: 4, of which 0 were waited for; matrix products, arithmetic and copies ran while one was open for 74% of the time, Pallas kernels for 0%

commit v1 on v0

v1 whole, which is shorter than its diff:
```python
import functools
import math

import jax
import jax.numpy as jnp
from jax import lax
from jax.experimental import pallas as pl
from jax.experimental.pallas import tpu as pltpu
from jax.sharding import PartitionSpec as P

HD = 128
MESH = pl.DeviceIdType.MESH
neg_fill = -1e30
eps_norm = 1e-06
F32 = jnp.float32
BF16 = jnp.bfloat16


def ceil_to(value, unit):
    return -(-value // unit) * unit


def kernel(
    sizes,
    order_ref,
    q_ref,
    k_ref,
    v_ref,
    ids_ref,
    table_ref,
    short_ref,
    long_ref,
    gain_ref,
    att_ref,
    hy_ref,
    kbuf,
    vbuf,
    qbuf,
    obuf,
    oland,
    ids_buf,
    table_buf,
    hot,
    feat_a,
    feat_b,
    feat_c,
    prod,
    taps_buf,
    mixed,
    squares,
    peak,
    total,
    acc,
    own_sem,
    pair_send,
    pair_recv,
    ids_send,
    ids_recv,
    ring_send,
    ring_recv,
    table_sem,
    sq_send,
    sq_recv,
    out_send,
    out_recv,
):
    n_ctx, n_grp, tile = sizes
    rows, width = q_ref.shape
    half_width = width // 2
    heads = half_width // HD
    half_rows = rows // 2
    channels = table_ref.shape[2]
    vocab = table_ref.shape[1]
    short_taps = short_ref.shape[1]
    groups, taps = long_ref.shape
    group_size = channels // groups
    units = channels // tile
    lead = hot.shape[0] - rows
    behind = lead - rows
    chips = n_ctx // 2
    far = chips // 2

    me = lax.axis_index("ctx")
    my_grp = lax.axis_index("grp")
    chip = me // 2
    core = me % 2

    def ring_of(c):
        return jnp.where(c % 2 == 0, c // 2, chips - 1 - c // 2)

    def chip_at(place):
        return jnp.where(place < far, 2 * place, 2 * (chips - 1 - place) + 1)

    place = ring_of(chip)
    sibling = chip * 2 + (1 - core)
    right = chip_at(lax.rem(place + 1, chips)) * 2 + core
    left = chip_at(lax.rem(place + chips - 1, chips)) * 2 + core
    after = [lax.rem(me + d, n_ctx) for d in (1, 2)]
    before = [lax.rem(me + n_ctx - d, n_ctx) for d in (1, 2)]
    peers = [lax.rem(my_grp + d, n_grp) for d in range(1, n_grp)]

    barrier = pltpu.get_barrier_semaphore()
    greet = [(t, my_grp) for t in [sibling, right, left] + after + before]
    greet += [(me, g) for g in peers]
    for target in greet:
        pl.semaphore_signal(barrier, inc=1, device_id=target, device_id_type=MESH)

    table_copies = []
    for j in range(units):
        cols = pl.ds(j * tile, tile)
        table_copies.append(
            pltpu.make_async_copy(
                table_ref.at[:, :, cols], table_buf.at[j], table_sem.at[j]
            )
        )
        table_copies[-1].start()
    mine = pl.ds(pl.multiple_of(core * half_width, half_width), half_width)
    theirs = pl.ds(pl.multiple_of((1 - core) * half_width, half_width), half_width)
    my_rows = pl.ds(pl.multiple_of(core * rows, rows), rows)
    pairs = ((k_ref, kbuf.at[0]), (v_ref, vbuf.at[0]), (q_ref, qbuf))
    own_copies = []
    for i, (src, dst) in enumerate(pairs):
        own_copies.append(
            pltpu.make_async_copy(src.at[:, mine], dst.at[my_rows, :], own_sem.at[i])
        )
        own_copies[-1].start()

    pl.semaphore_wait(barrier, len(greet))

    pair_copies = []
    for i, (src, dst) in enumerate(pairs):
        pair_copies.append(
            pltpu.make_async_remote_copy(
                src_ref=src.at[:, theirs],
                dst_ref=dst.at[my_rows, :],
                send_sem=pair_send.at[i],
                recv_sem=pair_recv.at[i],
                device_id=(sibling, my_grp),
                device_id_type=MESH,
            )
        )
        pair_copies[-1].start()
    ids_copies = []
    for i in range(2):
        ids_copies.append(
            pltpu.make_async_remote_copy(
                src_ref=ids_ref,
                dst_ref=ids_buf.at[i],
                send_sem=ids_send.at[i],
                recv_sem=ids_recv.at[i],
                device_id=(after[i], my_grp),
                device_id_type=MESH,
            )
        )
        ids_copies[-1].start()

    def ring_copy(to_right, is_key, step):
        buf = kbuf if is_key else vbuf
        if to_right:
            src, dst = step - 1, step
        else:
            src, dst = (chips - step + 1) % chips, chips - step
        slot = (0 if to_right else 1, 0 if is_key else 1, step - 1)
        return pltpu.make_async_remote_copy(
            src_ref=buf.at[src],
            dst_ref=buf.at[dst],
            send_sem=ring_send.at[slot],
            recv_sem=ring_recv.at[slot],
            device_id=(right if to_right else left, my_grp),
            device_id_type=MESH,
        )

    for i in range(2):
        own_copies[i].wait()
        pair_copies[i].wait_recv()
        ring_copy(True, i == 0, 1).start() if i == 0 or far > 1 else None
        ring_copy(False, i == 0, 1).start() if i == 1 or far > 1 else None

    def pass_on(step, first):
        last = step + 1 == far
        for to_right in (True, False):
            is_key = to_right == first
            ring_copy(to_right, is_key, step).wait_recv()
            if first or not last:
                ring_copy(to_right, is_key, step + 1).start()

    anti = lax.broadcasted_iota(jnp.int32, (taps, rows + taps), 1) + lax.broadcasted_iota(
        jnp.int32, (taps, rows + taps), 0
    )
    anti = jnp.where(anti == taps, 1.0, 0.0).astype(BF16)
    taps_buf[...] = jnp.dot(long_ref[...], anti, preferred_element_type=F32)

    for copy in ids_copies:
        copy.wait_recv()
    first_row = me * rows

    def one_hot(row_ids, offset):
        down = jnp.transpose(jnp.broadcast_to(row_ids, (HD, rows)))
        spot = lax.broadcasted_iota(jnp.int32, (rows, HD), 0) + (first_row + offset)
        down = jnp.where(spot >= 0, down, -1)
        lane = lax.broadcasted_iota(jnp.int32, (rows, HD), 1)
        parts = [
            jnp.where(down == lane + b * HD, 1.0, 0.0).astype(BF16) for b in range(vocab // HD)
        ]
        return jnp.concatenate(parts, axis=1)

    hot[0:behind, :] = one_hot(ids_buf[1], -2 * rows)[rows - behind :, :]
    hot[behind : behind + rows, :] = one_hot(ids_buf[0], -rows)
    hot[behind + rows :, :] = one_hot(ids_ref[...], 0)

    tail = rows + 16

    def short_rows(feat, stream, base, count, lanes, cols):
        out = None
        for k in range(short_taps):
            term = short_ref[stream, pl.ds(k, 1), cols] * feat[
                pl.ds(base - k, count), lanes
            ]
            out = term if out is None else out + term
        return out

    def hyena_unit(j, done):
        table_copies[j].wait()
        feat_a[...] = jnp.dot(hot[...], table_buf[j, 1], preferred_element_type=F32)
        feat_c[...] = jnp.dot(hot[...], table_buf[j, 3], preferred_element_type=F32)
        feat_b[...] = jnp.dot(
            hot[lead - 16 :, :], table_buf[j, 2], preferred_element_type=F32
        )
        residual = jnp.dot(hot[lead:, :], table_buf[j, 0], preferred_element_type=F32)
        mixed[:, j * tile : (j + 1) * tile] = residual
        step_rows = 64
        for sub in range(tile // HD):
            lanes = slice(sub * HD, (sub + 1) * HD)
            cols = slice(j * tile + sub * HD, j * tile + (sub + 1) * HD)
            for r in range(0, taps + rows, step_rows):
                base = lead - taps + r
                one = short_rows(feat_a, 0, base, step_rows, lanes, cols)
                three = short_rows(feat_c, 2, base, step_rows, lanes, cols)
                prod[r : r + step_rows, lanes] = (one * three).astype(BF16)
        done()
        for sub in range(tile // HD):
            lanes = slice(sub * HD, (sub + 1) * HD)
            cols = slice(j * tile + sub * HD, j * tile + (sub + 1) * HD)
            block = prod[:, lanes]
            lane_group = lax.broadcasted_iota(jnp.int32, (rows, HD), 1) // group_size
            per_sub = HD // group_size
            first_group = (j * tile + sub * HD) // group_size

            def add_group(g, conv):
                line = taps_buf[pl.ds(first_group + g, 1), :]
                wide = jnp.broadcast_to(line, (rows, rows + taps))
                band = pltpu.roll(wide, 0, 1, stride=1, stride_axis=0).astype(BF16)
                part = jnp.dot(band, block, preferred_element_type=F32)
                return jnp.where(lane_group == g, part, conv)

            conv = lax.fori_loop(
                0, per_sub, add_group, jnp.zeros((rows, HD), F32), unroll=True
            )
            two = short_rows(feat_b, 1, 16, rows, lanes, cols)
            whole = mixed[:, cols] + two * conv
            mixed[:, cols] = whole
            square = whole * whole
            if j == 0 and sub == 0:
                squares[0] = square
            else:
                squares[0] = squares[0] + square

    def positions(of_chip, shape, dim):
        at = lax.broadcasted_iota(jnp.int32, shape, dim)
        piece = at // half_rows
        start = jnp.full(shape, order_ref[of_chip * 4], jnp.int32)
        for b in range(1, 4):
            start = jnp.where(piece == b, order_ref[of_chip * 4 + b], start)
        return start * half_rows + at % half_rows

    scale = 1.0 / math.sqrt(HD)

    def attend(slot, start):
        owner = chip_at(lax.rem(place + chips - slot, chips))
        key_pos = positions(owner, (1, 2 * rows), 1)
        query_pos = positions(chip, (2 * rows, 1), 0)
        visible = key_pos <= query_pos
        for head in range(heads):
            cols = slice(head * HD, (head + 1) * HD)
            scores = lax.dot_general(
                qbuf[:, cols],
                kbuf[slot, :, cols],
                (((1,), (1,)), ((), ())),
                preferred_element_type=F32,
            )
            scores = jnp.where(visible, scores * scale, neg_fill)
            top = jnp.max(scores, axis=1, keepdims=True)
            if not start:
                old = peak[head]
                top = jnp.maximum(old, top)
            weights = jnp.where(visible, jnp.exp(scores - top), 0.0)
            mass = jnp.sum(weights, axis=1, keepdims=True)
            summed = jnp.dot(
                weights.astype(BF16), vbuf[slot, :, cols], preferred_element_type=F32
            )
            if not start:
                shrink = jnp.exp(old - top)
                mass = total[head] * shrink + mass
                summed = acc[head] * shrink + summed
            peak[head] = top
            total[head] = mass
            acc[head] = summed

    events = [(s, f) for s in range(1, far) for f in (True, False)]
    passed = []

    def next_event():
        if events:
            step, first = events.pop(0)
            pass_on(step, first)
            if not first:
                passed.append(step)

    def nothing():
        return None

    for j in range(units):
        hyena_unit(j, next_event if j % 2 == 0 else nothing)

    sq_copies = []
    for i, g in enumerate(peers):
        sq_copies.append(
            pltpu.make_async_remote_copy(
                src_ref=squares.at[0],
                dst_ref=squares.at[i + 1],
                send_sem=sq_send.at[i],
                recv_sem=sq_recv.at[i],
                device_id=(me, g),
                device_id_type=MESH,
            )
        )
        sq_copies[-1].start()

    next_event()
    own_copies[2].wait()
    pair_copies[2].wait_recv()
    attend(0, True)
    while events:
        for step in passed:
            attend(step, False)
            attend(chips - step, False)
        passed.clear()
        next_event()

    for copy in sq_copies:
        copy.wait_recv()
    sum_sq = squares[0]
    for i in range(len(peers)):
        sum_sq = sum_sq + squares[i + 1]
    mean = jnp.sum(sum_sq, axis=1, keepdims=True) / (channels * n_grp)
    inverse = lax.rsqrt(mean + eps_norm)
    hy_ref[...] = (mixed[...] * gain_ref[...] * inverse).astype(BF16)
    for step in passed:
        attend(step, False)
        attend(chips - step, False)

    ring_copy(True, True, far).wait_recv()
    ring_copy(False, False, far).wait_recv()
    attend(far, False)

    for head in range(heads):
        cols = slice(head * HD, (head + 1) * HD)
        obuf[:, cols] = (acc[head] / total[head]).astype(BF16)
    their_rows = pl.ds(pl.multiple_of((1 - core) * rows, rows), rows)
    back = pltpu.make_async_remote_copy(
        src_ref=obuf.at[their_rows, :],
        dst_ref=oland,
        send_sem=out_send,
        recv_sem=out_recv,
        device_id=(sibling, my_grp),
        device_id_type=MESH,
    )
    back.start()
    for copy in pair_copies + ids_copies + sq_copies:
        copy.wait_send()
    for step in range(1, far + 1):
        for to_right in (True, False):
            for is_key in (True, False):
                if step < far or to_right == is_key:
                    ring_copy(to_right, is_key, step).wait_send()
    kept = obuf[my_rows, :]
    back.wait()
    got = oland[...]
    att_ref[:, :half_width] = jnp.where(core == 0, kept, got)
    att_ref[:, half_width:] = jnp.where(core == 0, got, kept)


def body(
    n_ctx,
    n_grp,
    queries,
    keys,
    values,
    block_order,
    token_ids,
    stream_table,
    short_filter,
    long_filter,
    norm_gain,
):
    rows, width = queries.shape
    half_width = width // 2
    heads = half_width // HD
    channels = stream_table.shape[2]
    vocab = stream_table.shape[1]
    groups, taps = long_filter.shape
    lead = ceil_to(taps - 1 + short_filter.shape[1] - 1, 16)
    tile = math.gcd(channels, 256)
    units = channels // tile
    chips = n_ctx // 2
    far = chips // 2
    vmem = pl.BlockSpec(memory_space=pltpu.VMEM)
    dma = pltpu.SemaphoreType.DMA
    return pl.pallas_call(
        functools.partial(kernel, (n_ctx, n_grp, tile)),
        out_shape=(
            jax.ShapeDtypeStruct((rows, width), BF16),
            jax.ShapeDtypeStruct((rows, channels), BF16),
        ),
        in_specs=[
            pl.BlockSpec(memory_space=pltpu.SMEM),
            vmem,
            vmem,
            vmem,
            vmem,
            pl.BlockSpec(memory_space=pl.ANY),
            vmem,
            vmem,
            vmem,
        ],
        out_specs=(vmem, vmem),
        scratch_shapes=[
            pltpu.VMEM((chips, 2 * rows, half_width), BF16),
            pltpu.VMEM((chips, 2 * rows, half_width), BF16),
            pltpu.VMEM((2 * rows, half_width), BF16),
            pltpu.VMEM((2 * rows, half_width), BF16),
            pltpu.VMEM((rows, half_width), BF16),
            pltpu.VMEM((2, 1, rows), jnp.int32),
            pltpu.VMEM((units, 4, vocab, tile), BF16),
            pltpu.VMEM((lead + rows, vocab), BF16),
            pltpu.VMEM((lead + rows, tile), F32),
            pltpu.VMEM((rows + 16, tile), F32),
            pltpu.VMEM((lead + rows, tile), F32),
            pltpu.VMEM((rows + taps, tile), BF16),
            pltpu.VMEM((groups, rows + taps), F32),
            pltpu.VMEM((rows, channels), F32),
            pltpu.VMEM((n_grp, rows, HD), F32),
            pltpu.VMEM((heads, 2 * rows, 1), F32),
            pltpu.VMEM((heads, 2 * rows, 1), F32),
            pltpu.VMEM((heads, 2 * rows, HD), F32),
            dma((3,)),
            dma((3,)),
            dma((3,)),
            dma((2,)),
            dma((2,)),
            dma((2, 2, far)),
            dma((2, 2, far)),
            dma((units,)),
            dma((max(n_grp - 1, 1),)),
            dma((max(n_grp - 1, 1),)),
            dma,
            dma,
        ],
        compiler_params=pltpu.CompilerParams(
            collective_id=0, has_side_effects=True, vmem_limit_bytes=48 * 1024 * 1024
        ),
    )(
        block_order,
        queries,
        keys,
        values,
        token_ids.reshape(1, rows),
        stream_table,
        short_filter,
        long_filter,
        norm_gain.reshape(1, channels),
    )


def solution(mesh):
    placed = (
        P("ctx", "grp"),
        P("ctx", "grp"),
        P("ctx", "grp"),
        P(),
        P("ctx"),
        P(None, None, "grp"),
        P(None, None, "grp"),
        P("grp", None),
        P("grp"),
    )
    return jax.shard_map(
        functools.partial(body, mesh.shape["ctx"], mesh.shape["grp"]),
        mesh=mesh,
        in_specs=placed,
        out_specs=(P("ctx", "grp"), P("ctx", "grp")),
        check_vma=False,
    )
```

time: 153 us -> 45.1 us (0.29)
  local copies, waits for them, and re-layouts: 103 us -> 9.86 us
  Pallas kernels: 0 us -> 34.2 us
  matrix products: 14.3 us -> 0 us
  between operations: 14.3 us -> 0.66 us
  starting transfers between devices: 7.03 us -> 0 us
  other arithmetic: 6.48 us -> 0 us
  blocking collectives: 4.93 us -> 0 us
    gather x3 -> x0, local copies, waits for them, and re-layouts: 90.7 us -> none  [long_mix(): picked = long_filter[:, jnp.clip(lag_table, 0, tap_count - 1)]]
    pallas_call x0 -> x1, Pallas kernels: none -> 34.2 us  [body(): pl.pallas_call(functools.partial(kernel, (n_ctx, n_grp, tile)), out_shape...]
    dot_general x6 -> x0, matrix products: 14.3 us -> none  [the longest x2 4.06 us: attend_tile(): jnp.einsum('hqk,khd->qhd', weights.astype(jnp.bfloat16), values_tile, pre...]
    unnamed x12 -> x20, local copies, waits for them, and re-layouts: 2.05 us -> 9.86 us
    ppermute x2 -> x0, starting transfers between devices: 6.96 us -> none  [passed_along(): return lax.ppermute(block, axis, route)]
    psum x1 -> x0, blocking collectives: 4.93 us -> none  [body(): square_sum = lax.psum(jnp.sum(mixed * mixed, axis=1), 'grp')]
    all_gather x1 -> x0, local copies, waits for them, and re-layouts: 4 us -> none  [body(): values_piece = lax.all_gather(values, 'ctx', axis=0, tiled=True)]
    reduce_sum x5 -> x0, other arithmetic: 3.2 us -> none  [the longest x2 1.51 us: block_positions(): block_start = jnp.sum(jnp.where(hits, order[None, :], 0), axis=1)]
  transfers between devices with their start and end apart: 4 -> 0, of which waited for: 0 -> 0; matrix products, arithmetic and copies ran while one was open for 74% -> 0% of each run, Pallas kernels for 0% -> 0%
where the time goes in v1:
time: 45.1 us; the launch traced here: 44.7 us
  Pallas kernels  34.2 us (76%)
  local copies, waits for them, and re-layouts  9.86 us (22%)
  between operations  0.66 us (1%)
    pallas_call x1, Pallas kernels, body(): pl.pallas_call(functools.partial(kernel, (n_ctx, n_grp, tile)), out_shape...  34.2 us
    unnamed x20, local copies, waits for them, and re-layouts  9.86 us

profile of v1, /device:TPU:0, one launch (start us, length us, event | category | flops | bytes accessed | tf_op | source)
XLA Modules:
  0.0 44.7 jit_solution(15586109336102283587)
XLA Ops:
  0.6 0.0 copy-start
  0.6 2.2 %copy-done = bf16[4,512,1024]{2,1,0:T(8,128)(2,1)S(1)} copy-done((bf16[4,512,1024]{2,1,0:T(8,128)(2,1)S(1)}, bf16[4,512,1024]{2,1,0:T(8,128)(2,1)}, u32[]{:S(2)}) %copy-start) | copy-done | bytes 4194328
  2.8 0.0 copy-start.1
  2.8 0.9 %copy-done.1 = bf16[128,512]{1,0:T(8,128)(2,1)S(1)} copy-done((bf16[128,512]{1,0:T(8,128)(2,1)S(1)}, bf16[128,512]{1,0:T(8,128)(2,1)}, u32[]{:S(2)}) %copy-start.1) | copy-done | bytes 131096
  3.7 0.0 copy-start.2
  3.7 0.9 %copy-done.2 = bf16[128,512]{1,0:T(8,128)(2,1)S(1)} copy-done((bf16[128,512]{1,0:T(8,128)(2,1)S(1)}, bf16[128,512]{1,0:T(8,128)(2,1)}, u32[]{:S(2)}) %copy-start.2) | copy-done | bytes 131096
  4.6 0.0 copy-start.3
  4.6 0.9 %copy-done.3 = bf16[128,512]{1,0:T(8,128)(2,1)S(1)} copy-done((bf16[128,512]{1,0:T(8,128)(2,1)S(1)}, bf16[128,512]{1,0:T(8,128)(2,1)}, u32[]{:S(2)}) %copy-start.3) | copy-done | bytes 131096
  5.5 0.0 copy-start.4
  5.5 0.9 %copy-done.4 = f32[3,7,1024]{2,1,0:T(8,128)S(1)} copy-done((f32[3,7,1024]{2,1,0:T(8,128)S(1)}, f32[3,7,1024]{2,1,0:T(8,128)}, u32[]{:S(2)}) %copy-start.4) | copy-done | bytes 86040
  6.4 0.0 copy-start.5
  6.4 0.7 %copy-done.5 = bf16[64,128]{1,0:T(8,128)(2,1)S(1)} copy-done((bf16[64,128]{1,0:T(8,128)(2,1)S(1)}, bf16[64,128]{1,0:T(8,128)(2,1)}, u32[]{:S(2)}) %copy-start.5) | copy-done | bytes 16408
  7.1 0.0 copy-start.6
  7.1 0.7 %copy-done.6 = f32[1024]{0:T(1024)S(1)} copy-done((f32[1024]{0:T(1024)S(1)}, f32[1024]{0:T(1024)}, u32[]{:S(2)}) %copy-start.6) | copy-done | bytes 4120
  7.8 0.0 copy-start.7
  7.8 0.7 %copy-done.7 = s32[32]{0:T(128)S(1)} copy-done((s32[32]{0:T(128)S(1)}, s32[32]{0:T(128)}, u32[]{:S(2)}) %copy-start.7) | copy-done | bytes 152
  8.5 0.0 copy-start.8
  8.5 0.7 %copy-done.8 = s32[128]{0:T(128)S(1)} copy-done((s32[128]{0:T(128)S(1)}, s32[128]{0:T(128)}, u32[]{:S(2)}) %copy-start.8) | copy-done | bytes 536
  9.1 34.2 %shard_map.104 = (bf16[128,512]{1,0:T(8,128)(2,1)S(1)}, bf16[128,1024]{1,0:T(8,128)(2,1)S(1)}) custom-call(s32[32]{0:T(128)S(1)} %copy-done.7, bf16[128,512]{1,0:T(8,128)(2,1)S(1)} %copy-done.1, bf16[128,512]{1,0:T(8,128)(2,1)S(1)} %copy-done.2, bf16[128,512]{1,0:T(8,128)(2,1)S(1)} %copy-done.3, s32[1,128]{1,0:T(1,128)S(1)} %bitcast.3, ...), custom_call_target="tpu_custom_call" | custom-call | tf_op jit(solution)/shard_map/pallas_call | solution.py:419
  43.4 0.7 %copy.13 = bf16[128,512]{1,0:T(8,128)(2,1)} copy(bf16[128,512]{1,0:T(8,128)(2,1)S(1)} %get-tuple-element.4) | data formatting | bytes 262144
  44.0 0.7 %copy.14 = bf16[128,1024]{1,0:T(8,128)(2,1)} copy(bf16[128,1024]{1,0:T(8,128)(2,1)S(1)} %get-tuple-element.5) | data formatting | bytes 524288
Async XLA Ops:
  0.6 2.2 %copy-start = (bf16[4,512,1024]{2,1,0:T(8,128)(2,1)S(1)}, bf16[4,512,1024]{2,1,0:T(8,128)(2,1)}, u32[]{:S(2)}) copy-start(bf16[4,512,1024]{2,1,0:T(8,128)(2,1)} %table_ref.1) | copy-start | bytes 12582916
  2.8 0.9 %copy-start.1 = (bf16[128,512]{1,0:T(8,128)(2,1)S(1)}, bf16[128,512]{1,0:T(8,128)(2,1)}, u32[]{:S(2)}) copy-start(bf16[128,512]{1,0:T(8,128)(2,1)} %q_ref.1) | copy-start | bytes 393220
  3.7 0.9 %copy-start.2 = (bf16[128,512]{1,0:T(8,128)(2,1)S(1)}, bf16[128,512]{1,0:T(8,128)(2,1)}, u32[]{:S(2)}) copy-start(bf16[128,512]{1,0:T(8,128)(2,1)} %k_ref.1) | copy-start | bytes 393220
  4.6 0.9 %copy-start.3 = (bf16[128,512]{1,0:T(8,128)(2,1)S(1)}, bf16[128,512]{1,0:T(8,128)(2,1)}, u32[]{:S(2)}) copy-start(bf16[128,512]{1,0:T(8,128)(2,1)} %v_ref.1) | copy-start | bytes 393220
  5.5 0.9 %copy-start.4 = (f32[3,7,1024]{2,1,0:T(8,128)S(1)}, f32[3,7,1024]{2,1,0:T(8,128)}, u32[]{:S(2)}) copy-start(f32[3,7,1024]{2,1,0:T(8,128)} %short_ref.1) | copy-start | bytes 258052
  6.4 0.7 %copy-start.5 = (bf16[64,128]{1,0:T(8,128)(2,1)S(1)}, bf16[64,128]{1,0:T(8,128)(2,1)}, u32[]{:S(2)}) copy-start(bf16[64,128]{1,0:T(8,128)(2,1)} %long_ref.1) | copy-start | bytes 49156
  7.1 0.7 %copy-start.6 = (f32[1024]{0:T(1024)S(1)}, f32[1024]{0:T(1024)}, u32[]{:S(2)}) copy-start(f32[1024]{0:T(1024)} %param.17) | copy-start | bytes 12292
  7.8 0.7 %copy-start.7 = (s32[32]{0:T(128)S(1)}, s32[32]{0:T(128)}, u32[]{:S(2)}) copy-start(s32[32]{0:T(128)} %order_ref.1) | copy-start | bytes 388
  8.5 0.7 %copy-start.8 = (s32[128]{0:T(128)S(1)}, s32[128]{0:T(128)}, u32[]{:S(2)}) copy-start(s32[128]{0:T(128)} %param.13) | copy-start | bytes 1540

commit v2 on v1

--- a/solution.py
+++ b/solution.py
@@ -22,17 +22,23 @@
 
 def kernel(
     sizes,
-    order_ref,
+    order_in,
     q_ref,
     k_ref,
     v_ref,
+    ids_in,
+    table_ref,
+    short_in,
+    long_in,
+    gain_in,
+    att_ref,
+    hy_ref,
+    order_ref,
     ids_ref,
-    table_ref,
     short_ref,
     long_ref,
     gain_ref,
-    att_ref,
-    hy_ref,
+    small_sem,
     kbuf,
     vbuf,
     qbuf,
@@ -105,15 +111,6 @@
     for target in greet:
         pl.semaphore_signal(barrier, inc=1, device_id=target, device_id_type=MESH)
 
-    table_copies = []
-    for j in range(units):
-        cols = pl.ds(j * tile, tile)
-        table_copies.append(
-            pltpu.make_async_copy(
-                table_ref.at[:, :, cols], table_buf.at[j], table_sem.at[j]
-            )
-        )
-        table_copies[-1].start()
     mine = pl.ds(pl.multiple_of(core * half_width, half_width), half_width)
     theirs = pl.ds(pl.multiple_of((1 - core) * half_width, half_width), half_width)
     my_rows = pl.ds(pl.multiple_of(core * rows, rows), rows)
@@ -124,6 +121,22 @@
             pltpu.make_async_copy(src.at[:, mine], dst.at[my_rows, :], own_sem.at[i])
         )
         own_copies[-1].start()
+
+    small = ((ids_in, ids_ref), (order_in, order_ref), (long_in, long_ref))
+    small += ((short_in, short_ref), (gain_in, gain_ref))
+    small_copies = []
+    for i, (src, dst) in enumerate(small):
+        small_copies.append(pltpu.make_async_copy(src, dst, small_sem.at[i]))
+        small_copies[-1].start()
+    table_copies = []
+    for j in range(units):
+        cols = pl.ds(j * tile, tile)
+        table_copies.append(
+            pltpu.make_async_copy(
+                table_ref.at[:, :, cols], table_buf.at[j], table_sem.at[j]
+            )
+        )
+        table_copies[-1].start()
 
     pl.semaphore_wait(barrier, len(greet))
 
@@ -144,7 +157,7 @@
     for i in range(2):
         ids_copies.append(
             pltpu.make_async_remote_copy(
-                src_ref=ids_ref,
+                src_ref=ids_in,
                 dst_ref=ids_buf.at[i],
                 send_sem=ids_send.at[i],
                 recv_sem=ids_recv.at[i],
@@ -183,6 +196,9 @@
             ring_copy(to_right, is_key, step).wait_recv()
             if first or not last:
                 ring_copy(to_right, is_key, step + 1).start()
+
+    for copy in small_copies:
+        copy.wait()
 
     anti = lax.broadcasted_iota(jnp.int32, (taps, rows + taps), 1) + lax.broadcasted_iota(
         jnp.int32, (taps, rows + taps), 0
@@ -422,19 +438,15 @@
             jax.ShapeDtypeStruct((rows, width), BF16),
             jax.ShapeDtypeStruct((rows, channels), BF16),
         ),
-        in_specs=[
-            pl.BlockSpec(memory_space=pltpu.SMEM),
-            vmem,
-            vmem,
-            vmem,
-            vmem,
-            pl.BlockSpec(memory_space=pl.ANY),
-            vmem,
-            vmem,
-            vmem,
-        ],
+        in_specs=[pl.BlockSpec(memory_space=pltpu.HBM)] * 9,
         out_specs=(vmem, vmem),
         scratch_shapes=[
+            pltpu.SMEM(block_order.shape, jnp.int32),
+            pltpu.VMEM((1, rows), jnp.int32),
+            pltpu.VMEM(short_filter.shape, F32),
+            pltpu.VMEM(long_filter.shape, BF16),
+            pltpu.VMEM((1, channels), F32),
+            dma((5,)),
             pltpu.VMEM((chips, 2 * rows, half_width), BF16),
             pltpu.VMEM((chips, 2 * rows, half_width), BF16),
             pltpu.VMEM((2 * rows, half_width), BF16),
@@ -467,7 +479,7 @@
             dma,
         ],
         compiler_params=pltpu.CompilerParams(
-            collective_id=0, has_side_effects=True, vmem_limit_bytes=48 * 1024 * 1024
+            collective_id=0, has_side_effects=True, vmem_limit_bytes=64 * 1024 * 1024
         ),
     )(
         block_order,

time: 45.1 us -> 38.7 us (0.86)
  local copies, waits for them, and re-layouts: 9.86 us -> 3.24 us
  Pallas kernels: 34.2 us -> 34.7 us
    unnamed x20 -> x2, local copies, waits for them, and re-layouts: 9.86 us -> 3.24 us
    pallas_call x1, Pallas kernels: 34.2 us -> 34.7 us  [body(): pl.pallas_call(functools.partial(kernel, (n_ctx, n_grp, tile)), out_shape...]
where the time goes in v2:
time: 38.7 us; the launch traced here: 38.6 us
  Pallas kernels  34.7 us (90%)
  local copies, waits for them, and re-layouts  3.24 us (8%)
  between operations  0.64 us (2%)
    pallas_call x1, Pallas kernels, body(): pl.pallas_call(functools.partial(kernel, (n_ctx, n_grp, tile)), out_shape...  34.7 us
    unnamed x2, local copies, waits for them, and re-layouts  3.24 us

profile of v2, /device:TPU:0, one launch (start us, length us, event | category | flops | bytes accessed | tf_op | source)
XLA Modules:
  0.0 38.6 jit_solution(5804733910441796540)
XLA Ops:
  0.6 34.7 %shard_map.104 = (bf16[128,512]{1,0:T(8,128)(2,1)}, bf16[128,1024]{1,0:T(8,128)(2,1)}) custom-call(s32[32]{0:T(128)} %order_in.1, bf16[128,512]{1,0:T(8,128)(2,1)} %q_ref.1, bf16[128,512]{1,0:T(8,128)(2,1)} %k_ref.1, bf16[128,512]{1,0:T(8,128)(2,1)} %v_ref.1, s32[1,128]{1,0:T(1,128)} %bitcast.3, bf16[4,512,1024]{2,1,0:T(8,128)(2,1)} %table_ref.1, ...), custom_call_target="tpu_custom_call" | custom-call | tf_op jit(solution)/shard_map/pallas_call | solution.py:435
  35.3 1.6 %copy.13 = bf16[128,512]{1,0:T(8,128)(2,1)} copy(bf16[128,512]{1,0:T(8,128)(2,1)} %get-tuple-element.4) | data formatting | bytes 262144
  36.9 1.7 %copy.14 = bf16[128,1024]{1,0:T(8,128)(2,1)} copy(bf16[128,1024]{1,0:T(8,128)(2,1)} %get-tuple-element.5) | data formatting | bytes 524288

commit v3 on v2

--- a/solution.py
+++ b/solution.py
@@ -167,35 +167,44 @@
         )
         ids_copies[-1].start()
 
-    def ring_copy(to_right, is_key, step):
+    their_half = pl.ds(pl.multiple_of((1 - core) * rows, rows), rows)
+    halves = (my_rows, their_half)
+
+    def ring_copy(to_right, is_key, step, half):
         buf = kbuf if is_key else vbuf
         if to_right:
             src, dst = step - 1, step
         else:
             src, dst = (chips - step + 1) % chips, chips - step
-        slot = (0 if to_right else 1, 0 if is_key else 1, step - 1)
+        slot = (0 if to_right else 1, 0 if is_key else 1, 2 * (step - 1) + half)
         return pltpu.make_async_remote_copy(
-            src_ref=buf.at[src],
-            dst_ref=buf.at[dst],
+            src_ref=buf.at[src, halves[half], :],
+            dst_ref=buf.at[dst, halves[half], :],
             send_sem=ring_send.at[slot],
             recv_sem=ring_recv.at[slot],
             device_id=(right if to_right else left, my_grp),
             device_id_type=MESH,
         )
 
-    for i in range(2):
-        own_copies[i].wait()
-        pair_copies[i].wait_recv()
-        ring_copy(True, i == 0, 1).start() if i == 0 or far > 1 else None
-        ring_copy(False, i == 0, 1).start() if i == 1 or far > 1 else None
-
-    def pass_on(step, first):
-        last = step + 1 == far
-        for to_right in (True, False):
-            is_key = to_right == first
-            ring_copy(to_right, is_key, step).wait_recv()
-            if first or not last:
-                ring_copy(to_right, is_key, step + 1).start()
+    def send_on(to_right, is_key, step, half):
+        if step < far or to_right == is_key:
+            ring_copy(to_right, is_key, step, half).start()
+
+    for half in range(2):
+        for i in range(2):
+            if half == 0:
+                own_copies[i].wait()
+            else:
+                pair_copies[i].wait_recv()
+            send_on(True, i == 0, 1, half)
+            send_on(False, i == 0, 1, half)
+
+    def pass_on(step, half):
+        for order in (0, 1):
+            for to_right in (True, False):
+                is_key = to_right == (order == 0)
+                ring_copy(to_right, is_key, step, half).wait_recv()
+                send_on(to_right, is_key, step + 1, half)
 
     for copy in small_copies:
         copy.wait()
@@ -322,14 +331,14 @@
             total[head] = mass
             acc[head] = summed
 
-    events = [(s, f) for s in range(1, far) for f in (True, False)]
+    events = [(s, f) for s in range(1, far) for f in (0, 1)]
     passed = []
 
     def next_event():
         if events:
             step, first = events.pop(0)
             pass_on(step, first)
-            if not first:
+            if first:
                 passed.append(step)
 
     def nothing():
@@ -375,8 +384,9 @@
         attend(step, False)
         attend(chips - step, False)
 
-    ring_copy(True, True, far).wait_recv()
-    ring_copy(False, False, far).wait_recv()
+    for half in range(2):
+        ring_copy(True, True, far, half).wait_recv()
+        ring_copy(False, False, far, half).wait_recv()
     attend(far, False)
 
     for head in range(heads):
@@ -398,7 +408,8 @@
         for to_right in (True, False):
             for is_key in (True, False):
                 if step < far or to_right == is_key:
-                    ring_copy(to_right, is_key, step).wait_send()
+                    for half in range(2):
+                        ring_copy(to_right, is_key, step, half).wait_send()
     kept = obuf[my_rows, :]
     back.wait()
     got = oland[...]
@@ -470,8 +481,8 @@
             dma((3,)),
             dma((2,)),
             dma((2,)),
-            dma((2, 2, far)),
-            dma((2, 2, far)),
+            dma((2, 2, 2 * far)),
+            dma((2, 2, 2 * far)),
             dma((units,)),
             dma((max(n_grp - 1, 1),)),
             dma((max(n_grp - 1, 1),)),

time: 38.7 us -> 35.4 us (0.915)
  Pallas kernels: 34.7 us -> 31.3 us
    pallas_call x1, Pallas kernels: 34.7 us -> 31.3 us  [body(): pl.pallas_call(functools.partial(kernel, (n_ctx, n_grp, tile)), out_shape...]
where the time goes in v3:
time: 35.4 us; the launch traced here: 35.2 us
  Pallas kernels  31.3 us (88%)
  local copies, waits for them, and re-layouts  3.24 us (9%)
  between operations  0.64 us (2%)
    pallas_call x1, Pallas kernels, body(): pl.pallas_call(functools.partial(kernel, (n_ctx, n_grp, tile)), out_shape...  31.3 us
    unnamed x2, local copies, waits for them, and re-layouts  3.24 us

profile of v3, /device:TPU:0, one launch (start us, length us, event | category | flops | bytes accessed | tf_op | source)
XLA Modules:
  0.0 35.2 jit_solution(3141057046612506852)
XLA Ops:
  0.6 31.3 %shard_map.104 = (bf16[128,512]{1,0:T(8,128)(2,1)}, bf16[128,1024]{1,0:T(8,128)(2,1)}) custom-call(s32[32]{0:T(128)} %order_in.1, bf16[128,512]{1,0:T(8,128)(2,1)} %q_ref.1, bf16[128,512]{1,0:T(8,128)(2,1)} %k_ref.1, bf16[128,512]{1,0:T(8,128)(2,1)} %v_ref.1, s32[1,128]{1,0:T(1,128)} %bitcast.3, bf16[4,512,1024]{2,1,0:T(8,128)(2,1)} %table_ref.1, ...), custom_call_target="tpu_custom_call" | custom-call | tf_op jit(solution)/shard_map/pallas_call | solution.py:446
  32.0 1.6 %copy.13 = bf16[128,512]{1,0:T(8,128)(2,1)} copy(bf16[128,512]{1,0:T(8,128)(2,1)} %get-tuple-element.4) | data formatting | bytes 262144
  33.5 1.7 %copy.14 = bf16[128,1024]{1,0:T(8,128)(2,1)} copy(bf16[128,1024]{1,0:T(8,128)(2,1)} %get-tuple-element.5) | data formatting | bytes 524288
